TPU v7x, 128 devices: a whole 4x4x4 slice. The times are simulated.
128 devices in a mesh: graph: 32 (over z, y, core), mp: 4 (over x).
Axes of the slice: x: 4, y: 4, z: 4, core: 2. Of those that a mesh axis runs over, the one named last changes fastest.
Arguments:
- node_features: bfloat16 [65536, 512], P('graph'), may hold values from -6 to 6
- w_qkv: bfloat16 [3, 512, 512], P(None, None, 'mp'), may hold values from -0.25 to 0.25
- w_out: bfloat16 [512, 512], P('mp'), may hold values from -0.25 to 0.25
- head_scale: float32 [8], P('mp'), may hold values from 1 to 100
- norm_gain: float32 [512], replicated, may hold values from 0.1 to 1.9
- router: bfloat16 [512, 64], replicated, may hold values from -0.5 to 0.5
- w_gate: bfloat16 [64, 512, 2048], P('graph', None, 'mp'), may hold values from -0.25 to 0.25
- w_up: bfloat16 [64, 512, 2048], P('graph', None, 'mp'), may hold values from -0.25 to 0.25
- w_down: bfloat16 [64, 2048, 512], P('graph', 'mp'), may hold values from -0.25 to 0.25
- neighbor_blocks: int32 [512, 12], P('graph'), may hold values from 0 to 511, as said below
- expert_ids: int32 [65536, 1], P('graph'), may hold values from 0 to 63; in each aligned block of 2048 rows (0 to 2047, 2048 to 4095, ...) at most 96 rows name the same one
Outputs:
- attn_out: bfloat16 [65536, 512], P('graph', 'mp')
- layer_out: bfloat16 [65536, 512], P('graph', 'mp')
Inputs may be any that keep to these rules, and one draw needn't show every extreme that they name: `neighbor_blocks`: row b lists distinct blocks: b itself, 3 other blocks of the same index of graph (blocks of part p are p * 16 to p * 16 + 15), then 8 blocks of other parts. Among all rows of one part, at most 2 distinct blocks come from any one other part, and every part reaches 2 from some other part. `expert_ids`: among the rows of one index of graph, at most 96 name one expert, a bound that some block reaches.
All inputs are finite; a program needn't handle non-finite values.
Results may differ from a plain program's by a relative error of at most 0.012.
The roundings to bfloat16 on the way count: a program that leaves them out, or rounds other values in their place, can miss the bound.
Values may be sent and summed in bfloat16 or wider, within the bound.
No kernel may reach another device: no remote copies, remote signals or barrier semaphores. Data moves between devices by JAX's collectives and lax.ppermute only.
A program may use at most 128 MiB of HBM per device.

v0:
```python
import math
import jax
import jax.numpy as jnp
from jax import lax
from jax.sharding import PartitionSpec as P

HEAD_DIM = 64
ROWS_BLK = 128
CAP_H = 2


def unit_rms(values):
    return values * lax.rsqrt(jnp.mean(values * values, axis=-1, keepdims=True) + 1e-06)


def make_work(gate_weights, up_weights, down_weights, tokens):
    gate_part = jnp.einsum(
        "gesd,edf->gesf", tokens, gate_weights, preferred_element_type=jnp.float32
    )
    up_part = jnp.einsum("gesd,edf->gesf", tokens, up_weights, preferred_element_type=jnp.float32)
    hidden = (jax.nn.silu(gate_part) * up_part).astype(jnp.bfloat16)
    return jnp.einsum("gesf,efd->gesd", hidden, down_weights, preferred_element_type=jnp.float32)


def on_device(
    node_features,
    w_qkv,
    w_out,
    head_scale,
    norm_gain,
    router,
    w_gate,
    w_up,
    w_down,
    neighbor_blocks,
    expert_ids,
):
    graph_count = lax.axis_size("graph")
    own_part = lax.axis_index("graph")
    column_start = lax.axis_index("mp") * w_qkv.shape[2]
    rows = node_features.shape[0]
    width = node_features.shape[1]
    local_width = w_qkv.shape[2]
    local_heads = local_width // HEAD_DIM
    blocks = rows // ROWS_BLK
    query = jnp.dot(node_features, w_qkv[0], preferred_element_type=jnp.float32).reshape(
        rows, local_heads, HEAD_DIM
    )
    keys = jnp.dot(node_features, w_qkv[1], preferred_element_type=jnp.float32).reshape(
        rows, local_heads, HEAD_DIM
    )
    values = jnp.dot(node_features, w_qkv[2], preferred_element_type=jnp.float32)
    scaled = (unit_rms(query) * (head_scale / math.sqrt(HEAD_DIM))[None, :, None]).astype(
        jnp.bfloat16
    )
    key_unit = unit_rms(keys).astype(jnp.bfloat16).reshape(blocks, ROWS_BLK, local_width)
    value_rows = values.astype(jnp.bfloat16).reshape(blocks, ROWS_BLK, local_width)
    key_value = jnp.concatenate([key_unit, value_rows], axis=2)
    entries = neighbor_blocks.reshape(-1)
    owner = entries // blocks
    local_index = entries % blocks
    listed = jnp.arange(entries.shape[0], dtype=jnp.int32)
    repeated = jnp.any(
        (entries[:, None] == entries[None, :]) & (listed[None, :] < listed[:, None]), axis=1
    )
    wanted = (owner != own_part) & jnp.logical_not(repeated)
    part_ids = jnp.arange(graph_count, dtype=jnp.int32)
    owner_hit = ((owner[:, None] == part_ids[None, :]) & wanted[:, None]).astype(jnp.int32)
    position = jnp.sum((jnp.cumsum(owner_hit, axis=0) - owner_hit) * owner_hit, axis=1)
    slot_hit = (position[:, None] == jnp.arange(CAP_H, dtype=jnp.int32)[None, :]).astype(jnp.int32)
    requests = (
        jnp.sum(
            owner_hit[:, :, None] * slot_hit[:, None, :] * (local_index + 1)[:, None, None], axis=0
        )
        - 1
    )
    incoming = lax.all_to_all(requests, "graph", split_axis=0, concat_axis=0, tiled=True)
    outgoing = key_value[jnp.maximum(incoming, 0)]
    halo_rows = lax.all_to_all(outgoing, "graph", split_axis=0, concat_axis=0, tiled=True)
    halo_ids = jnp.where(requests >= 0, part_ids[:, None] * blocks + requests, -1).reshape(-1)
    pool_ids = jnp.concatenate([own_part * blocks + jnp.arange(blocks, dtype=jnp.int32), halo_ids])
    key_pool = jnp.concatenate(
        [key_value, halo_rows.reshape(-1, ROWS_BLK, 2 * local_width)], axis=0
    )
    pool_slots = jnp.arange(pool_ids.shape[0], dtype=jnp.int32)
    slot_index = jnp.sum(
        jnp.where(
            neighbor_blocks[:, :, None] == pool_ids[None, None, :], pool_slots[None, None, :], 0
        ),
        axis=2,
    )
    gathered = key_pool[slot_index].reshape(blocks, -1, 2 * local_width)
    key_part = gathered[:, :, :local_width].reshape(blocks, -1, local_heads, HEAD_DIM)
    value_part = gathered[:, :, local_width:].reshape(blocks, -1, local_heads, HEAD_DIM)
    query_blocks = scaled.reshape(blocks, ROWS_BLK, local_heads, HEAD_DIM)
    scores = jnp.einsum(
        "bqhd,bkhd->bhqk", query_blocks, key_part, preferred_element_type=jnp.float32
    )
    largest = jnp.max(scores, axis=-1, keepdims=True)
    expo = jnp.exp(scores - largest)
    weights = (expo / jnp.sum(expo, axis=-1, keepdims=True)).astype(jnp.bfloat16)
    attended = jnp.einsum(
        "bhqk,bkhd->bqhd", weights, value_part, preferred_element_type=jnp.float32
    )
    attended = attended.astype(jnp.bfloat16).reshape(rows, local_width)
    partial_value = jnp.dot(attended, w_out, preferred_element_type=jnp.float32)
    total = lax.psum(partial_value, "mp")
    mixed = node_features.astype(jnp.float32) + total
    normed = (unit_rms(mixed) * norm_gain).astype(jnp.bfloat16)
    attn_cols = lax.dynamic_slice_in_dim(total, column_start, local_width, 1)
    mixed_cols = lax.dynamic_slice_in_dim(mixed, column_start, local_width, 1)
    experts = router.shape[1]
    capacity = 3 * rows // experts
    routed = expert_ids[:, 0]
    chosen = routed[:, None] == jnp.arange(experts, dtype=jnp.int32)[None, :]
    logits = jnp.dot(normed, router, preferred_element_type=jnp.float32)
    gate = jax.nn.sigmoid(jnp.sum(jnp.where(chosen, logits, 0.0), axis=1))
    row_ids = jnp.arange(rows, dtype=jnp.int32)
    earlier = (row_ids[:, None] > row_ids[None, :]).astype(jnp.bfloat16)
    before = jnp.dot(earlier, chosen.astype(jnp.bfloat16), preferred_element_type=jnp.float32)
    rank_in = jnp.sum(jnp.where(chosen, before, 0.0), axis=1).astype(jnp.int32)
    target = routed * capacity + rank_in
    buffer = jnp.zeros((experts * capacity, width), jnp.bfloat16).at[target].set(normed)
    buffer = buffer.reshape(graph_count, w_gate.shape[0], capacity, width)
    produced = make_work(
        w_gate,
        w_up,
        w_down,
        lax.all_to_all(buffer, "graph", split_axis=0, concat_axis=0, tiled=True),
    )
    back = lax.all_to_all(
        produced.astype(jnp.bfloat16), "graph", split_axis=0, concat_axis=0, tiled=True
    ).astype(produced.dtype)
    mine = back.reshape(-1, width)[target]
    expert_cols = lax.psum_scatter(
        mine.astype(jnp.bfloat16), "mp", scatter_dimension=1, tiled=True
    ).astype(jnp.float32)
    layer_out = (mixed_cols + gate[:, None] * expert_cols).astype(jnp.bfloat16)
    return (attn_cols.astype(jnp.bfloat16), layer_out)


def solution(mesh):
    placed = (
        P("graph", None),
        P(None, None, "mp"),
        P("mp", None),
        P("mp"),
        P(),
        P(),
        P("graph", None, "mp"),
        P("graph", None, "mp"),
        P("graph", "mp", None),
        P("graph", None),
        P("graph", None),
    )
    return jax.shard_map(
        on_device,
        mesh=mesh,
        in_specs=placed,
        out_specs=(P("graph", "mp"), P("graph", "mp")),
        check_vma=False,
    )
```

profile of v0, /device:TPU:1, one launch (start us, length us, event | category | flops | bytes accessed | tf_op | source)
XLA Modules:
  0.0 512.2 jit_solution(45271411930314655)
XLA Ops:
  10.1 9.6 %all-to-all-start = ((s32[32,1,2]{2,1,0:T(1,128)}), s32[32,1,2]{2,1,0:T(1,128)S(1)}, u32[]{:S(2)}, u32[]{:S(2)}) async-start(s32[32,1,2]{2,1,0:T(1,128)} %copy.52), calls=%async_computation | async-start | bytes 32768 | tf_op jit(solution)/shard_map/all_to_all | solution.py:77
  20.8 2.3 convolution_convert_fusion
  23.2 2.6 multiply_reduce_fusion.2
  27.3 2.8 gather_fusion
  30.1 7.6 %all-to-all-start.1 = ((bf16[32,2,128,256]{3,2,1,0:T(8,128)(2,1)}), bf16[32,2,128,256]{3,2,1,0:T(8,128)(2,1)}, u32[]{:S(2)}, u32[]{:S(2)}) async-start(bf16[32,2,128,256]{3,2,1,0:T(8,128)(2,1)} %bitcast.145), calls=%async_computation.1 | async-start | bytes 8388608 | tf_op jit(solution)/shard_map/all_to_all | solution.py:79
  39.0 1.9 multiply_reduce_fusion.1
  40.9 47.0 %all-to-all-done.1 = bf16[32,2,128,256]{3,2,1,0:T(8,128)(2,1)} async-done(((bf16[32,2,128,256]{3,2,1,0:T(8,128)(2,1)}), bf16[32,2,128,256]{3,2,1,0:T(8,128)(2,1)}, u32[]{:S(2)}, u32[]{:S(2)}) %all-to-all-start.1) | async-done | bytes 4194336 | tf_op jit(solution)/shard_map/all_to_all | solution.py:79
  87.9 5.5 %pad_maximum_fusion = bf16[80,128,256]{2,1,0:T(8,128)(2,1)} fusion(bf16[64,128,256]{2,1,0:T(8,128)(2,1)} %bitcast.9, bf16[16,128,128]{2,1,0:T(8,128)(2,1)} %bitcast.151, bf16[16,128,128]{2,1,0:T(8,128)(2,1)} %copy-done.3), kind=kLoop, calls=%fused_computation.24 | loop fusion | flops 15728640 | bytes 10485760 | tf_op jit(solution)/shard_map/concatenate | solution.py:82
  93.4 10.7 %gather_fusion.1 = bf16[192,128,256]{2,1,0:T(8,128)(2,1)} fusion(bf16[80,128,256]{2,1,0:T(8,128)(2,1)} %pad_maximum_fusion, s32[1024]{0:T(1024)S(1)} %pad_clamp_fusion), kind=kCustom, calls=%fused_computation.1 | custom fusion | bytes 25166592 | tf_op jit(solution)/shard_map/gather | solution.py:92
  104.2 11.7 %fusion.71 = (bf16[16,1536,128]{2,1,0:T(8,128)(2,1)}, bf16[16,1536,128]{2,1,0:T(8,128)(2,1)}) fusion(bf16[16,1536,256]{2,1,0:T(8,128)(2,1)} %bitcast.143), kind=kLoop, calls=%fused_computation.114 | loop fusion | bytes 25165824 | tf_op jit(solution)/shard_map/slice | solution.py:93
  115.9 8.7 %copy.58 = bf16[16,1536,128]{1,2,0:T(8,128)(2,1)} copy(bf16[16,1536,128]{2,1,0:T(8,128)(2,1)} %get-tuple-element.6) | data formatting | bytes 12582912 | tf_op jit(solution)/shard_map/slice | solution.py:93
  124.5 8.6 %copy.56 = bf16[16,1536,128]{1,2,0:T(8,128)(2,1)} copy(bf16[16,1536,128]{2,1,0:T(8,128)(2,1)} %get-tuple-element.7) | data formatting | bytes 12582912 | tf_op jit(solution)/shard_map/slice | solution.py:94
  133.2 7.8 %fusion.72 = f32[16,2,128]{2,1,0:T(2,128)S(1)} fusion(bf16[16,1536,2,64]{1,3,2,0:T(8,128)(2,1)} %bitcast.147, f32[2048,2,64]{0,2,1:T(8,128)} %get-tuple-element.15, f32[2]{0:T(128)S(1)} %broadcast_multiply_fusion, f32[2048,2]{0,1:T(2,128)S(1)} %add_rsqrt_fusion), kind=kOutput, calls=%fused_computation.115 | convolution fusion | flops 818677248 | bytes 7372808 | tf_op jit(solution)/shard_map/sub | solution.py:100
  141.0 12.9 %fusion.29 = bf16[16,128,2,64]{1,3,2,0:T(8,128)(2,1)} fusion(bf16[16,1536,2,64]{1,3,2,0:T(8,128)(2,1)} %bitcast.149, f32[16,2,128]{2,1,0:T(2,128)S(1)} %fusion.72, bf16[16,1536,2,64]{1,3,2,0:T(8,128)(2,1)} %bitcast.148, f32[2048,2,64]{0,2,1:T(8,128)} %get-tuple-element.15, f32[2]{0:T(128)S(1)} %broadcast_multiply_fusion, f32[2048,2]{0,1:T(2,128)S(1)} %add_rsqrt_fusion), kind=kOutput, calls=%fused_computation.39 | convolution fusion | flops 1630541312 | bytes 14188552 | tf_op jit(solution)/shard_map/bhqk,bkhd->bqhd/dot_general | solution.py:102
  155.3 2.7 fusion.37
  158.0 1.7 fusion.31
  159.7 90.8 %all-reduce.3.cloned.1.call-done = f32[2048,512]{1,0:T(8,128)} async-done(((f32[2048,512]{1,0:T(8,128)}), f32[2048,512]{1,0:T(8,128)}) %all-reduce.3.cloned.1.call-update) | async-done | bytes 4194320 | tf_op jit(solution)/shard_map/psum | solution.py:107
  250.5 4.7 multiply_reduce_fusion
  255.2 14.8 %scatter_custom_fusion = bf16[6144,512]{1,0:T(8,128)(2,1)} fusion(s32[2048]{0:T(1024)S(1)} %bitcast.160, bf16[]{:T(256)} %constant.85.clone.1, f32[2048,512]{1,0:T(8,128)} %get-tuple-element.3, f32[512]{0:T(512)S(1)} %copy-done.9, f32[2048]{0:T(1024)S(1)} %add_rsqrt_fusion.2), kind=kCustom, calls=%fused_computation.28 | custom fusion | flops 3145728 | bytes 10496002 | tf_op jit(solution)/shard_map/scatter | solution.py:123
  270.0 81.1 %all_to_all.21 = bf16[32,2,96,512]{3,2,1,0:T(8,128)(2,1)S(1)} all-to-all(bf16[32,2,96,512]{3,2,1,0:T(8,128)(2,1)} %bitcast.144), channel_id=1, replica_groups=mesh['graph'=32,'mp'=4] {'graph'}, dimensions={0} | all-to-all | bytes 12582912 | tf_op jit(solution)/shard_map/all_to_all | solution.py:129
  351.0 2.6 copy-done.2
  353.6 6.5 %fusion.9 = f32[2,32,96,512]{3,2,1,0:T(8,128)} fusion(bf16[32,2,96,512]{3,2,1,0:T(8,128)(2,1)S(1)} %all_to_all.21, bf16[2,512,512]{2,1,0:T(8,128)(2,1)S(1)} %copy-done), kind=kOutput, calls=%fused_computation.20 | convolution fusion | flops 3221225472 | bytes 19922944 | tf_op jit(solution)/shard_map/gesd,edf->gesf/dot_general | solution.py:20
  360.1 14.0 %convert_bitcast_fusion = bf16[32,2,96,512]{3,2,0,1:T(8,128)(2,1)} fusion(f32[2,32,96,512]{3,2,1,0:T(8,128)} %fusion.9, bf16[32,2,96,512]{3,2,1,0:T(8,128)(2,1)} %copy-done.2, bf16[2,512,512]{2,1,0:T(8,128)(2,1)S(1)} %copy-done.10, bf16[2,512,512]{2,1,0:T(8,128)(2,1)S(1)} %copy-done.11), kind=kOutput, calls=%fused_computation.18 | convolution fusion | flops 6464471040 | bytes 27262976 | tf_op jit(solution)/shard_map/gesf,efd->gesd/dot_general | solution.py:22
  374.1 6.2 %copy.63 = bf16[32,2,96,512]{3,2,1,0:T(8,128)(2,1)} copy(bf16[32,2,96,512]{3,2,0,1:T(8,128)(2,1)} %convert_bitcast_fusion) | data formatting | bytes 12582912 | tf_op jit(solution)/shard_map/convert_element_type | solution.py:132
  380.2 4.9 all-to-all-start.3
  385.2 73.0 %all-to-all-done.3 = bf16[32,2,96,512]{3,2,1,0:T(8,128)(2,1)} async-done(((bf16[32,2,96,512]{3,2,1,0:T(8,128)(2,1)}), bf16[32,2,96,512]{3,2,1,0:T(8,128)(2,1)}, u32[]{:S(2)}, u32[]{:S(2)}) %all-to-all-start.3) | async-done | bytes 6291488 | tf_op jit(solution)/shard_map/all_to_all | solution.py:131
  458.2 11.2 %gather_fusion.2 = bf16[2048,512]{1,0:T(8,128)(2,1)S(1)} fusion(bf16[6144,512]{1,0:T(8,128)(2,1)} %bitcast.118, s32[2048]{0:T(1024)S(1)} %broadcast_clamp_fusion), kind=kCustom, calls=%fused_computation.2 | custom fusion | bytes 4202496 | tf_op jit(solution)/shard_map/gather | solution.py:134
  469.4 2.5 copy.67
  471.9 3.1 fusion.30
  475.0 2.1 dynamic-slice_convert_fusion
  477.1 24.6 %reduce-scatter.4.cloned.1.call-done = bf16[128,2048]{1,0:T(8,128)(2,1)} async-done(((bf16[512,2048]{1,0:T(8,128)(2,1)}), bf16[128,2048]{1,0:T(8,128)(2,1)}) %reduce-scatter.4.cloned.1.call-update) | async-done | bytes 524304
  502.9 2.4 add_convert_fusion
  (78 shorter events, 9.5 us)
Async XLA Ops:
  7.2 346.5 %copy-start = (bf16[2,512,512]{2,1,0:T(8,128)(2,1)S(1)}, bf16[2,512,512]{2,1,0:T(8,128)(2,1)}, u32[]{:S(2)}) copy-start(bf16[2,512,512]{2,1,0:T(8,128)(2,1)} %param.18) | copy-start | bytes 3145732
  10.1 16.6 %all-to-all-start = ((s32[32,1,2]{2,1,0:T(1,128)}), s32[32,1,2]{2,1,0:T(1,128)S(1)}, u32[]{:S(2)}, u32[]{:S(2)}) async-start(s32[32,1,2]{2,1,0:T(1,128)} %copy.52), calls=%async_computation | async-start | bytes 32768 | tf_op jit(solution)/shard_map/all_to_all | solution.py:77
  23.1 3.7 copy-start.4
  26.5 0.8 copy-start.3
  30.1 7.8 %copy-start.8 = (s32[16,12]{1,0:T(8,128)S(1)}, s32[16,12]{1,0:T(8,128)}, u32[]{:S(2)}) copy-start(s32[16,12]{1,0:T(8,128)} %param.20) | copy-start | bytes 2308
  30.1 8.9 %copy-start.12 = (f32[2]{0:T(128)S(1)}, f32[2]{0:T(128)}, u32[]{:S(2)}) copy-start(f32[2]{0:T(128)} %param.14) | copy-start | bytes 28
  30.1 8.9 %copy-start.1 = (bf16[2048,512]{1,0:T(8,128)(2,1)S(1)}, bf16[2048,512]{1,0:T(8,128)(2,1)}, u32[]{:S(2)}) copy-start(bf16[2048,512]{1,0:T(8,128)(2,1)} %param.11) | copy-start | bytes 6291460
  30.1 57.8 %all-to-all-start.1 = ((bf16[32,2,128,256]{3,2,1,0:T(8,128)(2,1)}), bf16[32,2,128,256]{3,2,1,0:T(8,128)(2,1)}, u32[]{:S(2)}, u32[]{:S(2)}) async-start(bf16[32,2,128,256]{3,2,1,0:T(8,128)(2,1)} %bitcast.145), calls=%async_computation.1 | async-start | bytes 8388608 | tf_op jit(solution)/shard_map/all_to_all | solution.py:79
  37.6 212.9 %all-reduce.3.cloned.1.call-start = ((), (), s32[]{:S(2)}) async-start(), calls=%async_computation.5 | async-start | bytes 8388608 | tf_op jit(solution)/shard_map/psum | solution.py:107
  141.0 14.3 %copy-start.5 = (bf16[128,512]{1,0:T(8,128)(2,1)S(1)}, bf16[128,512]{1,0:T(8,128)(2,1)}, u32[]{:S(2)}) copy-start(bf16[128,512]{1,0:T(8,128)(2,1)} %param.13) | copy-start | bytes 393220
  153.9 4.1 copy-start.7
  159.6 95.6 %copy-start.9 = (f32[512]{0:T(512)S(1)}, f32[512]{0:T(512)}, u32[]{:S(2)}) copy-start(f32[512]{0:T(512)} %param.15) | copy-start | bytes 6148
  351.0 2.6 copy-start.2
  353.6 6.5 %copy-start.10 = (bf16[2,512,512]{2,1,0:T(8,128)(2,1)S(1)}, bf16[2,512,512]{2,1,0:T(8,128)(2,1)}, u32[]{:S(2)}) copy-start(bf16[2,512,512]{2,1,0:T(8,128)(2,1)} %param.19) | copy-start | bytes 3145732
  353.6 6.5 %copy-start.11 = (bf16[2,512,512]{2,1,0:T(8,128)(2,1)S(1)}, bf16[2,512,512]{2,1,0:T(8,128)(2,1)}, u32[]{:S(2)}) copy-start(bf16[2,512,512]{2,1,0:T(8,128)(2,1)} %param.17) | copy-start | bytes 3145732
  380.2 77.9 %all-to-all-start.3 = ((bf16[32,2,96,512]{3,2,1,0:T(8,128)(2,1)}), bf16[32,2,96,512]{3,2,1,0:T(8,128)(2,1)}, u32[]{:S(2)}, u32[]{:S(2)}) async-start(bf16[32,2,96,512]{3,2,1,0:T(8,128)(2,1)} %copy.63), calls=%async_computation.3 | async-start | bytes 12582912 | tf_op jit(solution)/shard_map/all_to_all | solution.py:131
  385.1 116.5 %reduce-scatter.4.cloned.1.call-start = ((), (), s32[]{:S(2)}) async-start(), calls=%async_computation.6 | async-start | bytes 2621440
  469.4 2.5 copy-start.6
Sparse Core Ops, SparseCore 0:
  158.1 92.3 all-reduce.2
  472.0 29.5 reduce-scatter.3
where the time goes:
time: 513 us; the launch traced here: 512 us
  waiting for transfers between devices  235 us (46%)
  blocking collectives  81.1 us (16%)
  local copies, waits for them, and re-layouts  74.3 us (14%)
  matrix products  55.3 us (11%)
  other arithmetic  29.3 us (6%)
  starting transfers between devices  22.3 us (4%)
  between operations  14.5 us (3%)
    psum x1, waiting for transfers between devices, on_device(): total = lax.psum(partial_value, 'mp')  90.8 us
    all_to_all x1, blocking collectives, on_device(): lax.all_to_all(buffer, 'graph', split_axis=0, concat_axis=0, tiled=True)  81.1 us
    all_to_all x1, waiting for transfers between devices, on_device(): lax.all_to_all(produced.astype(jnp.bfloat16), 'graph', split_axis=0, conc...  73 us
    all_to_all x1, waiting for transfers between devices, on_device(): lax.all_to_all(outgoing, 'graph', split_axis=0, concat_axis=0, tiled=True)  47 us
    unnamed x3, waiting for transfers between devices  24.6 us
    slice x2, local copies, waits for them, and re-layouts, on_device(): gathered[:, :, :local_width].reshape(blocks, -1, local_heads, HEAD_DIM)  20.4 us
    scatter x1, other arithmetic, on_device(): jnp.zeros((experts * capacity, width), jnp.bfloat16).at[target].set(normed)  14.8 us
    dot_general x1, matrix products, make_work(): jnp.einsum('gesf,efd->gesd', hidden, down_weights, preferred_element_type...  14 us
  transfers between devices with their start and end apart: 5, of which 4 were waited for; matrix products, arithmetic and copies ran while one was open for 3% of the time, Pallas kernels for 0%

commit v1 on v0

--- a/solution.py
+++ b/solution.py
@@ -104,7 +104,9 @@
     )
     attended = attended.astype(jnp.bfloat16).reshape(rows, local_width)
     partial_value = jnp.dot(attended, w_out, preferred_element_type=jnp.float32)
-    total = lax.psum(partial_value, "mp")
+    total = partial_value
+    for hop in (1, 2):
+        total = total + lax.ppermute(total, "mp", [(dev, dev ^ hop) for dev in range(4)])
     mixed = node_features.astype(jnp.float32) + total
     normed = (unit_rms(mixed) * norm_gain).astype(jnp.bfloat16)
     attn_cols = lax.dynamic_slice_in_dim(total, column_start, local_width, 1)

time: 513 us -> 615 us (1.20)
  waiting for transfers between devices: 235 us -> 317 us
  local copies, waits for them, and re-layouts: 74.3 us -> 99.7 us
  other arithmetic: 29.3 us -> 18.2 us
  blocking collectives: 81.1 us -> 87.9 us
    ppermute x0 -> x2, waiting for transfers between devices: none -> 170 us  [on_device(): lax.ppermute(total, 'mp', [(dev, dev ^ hop) for dev in range(4)])]
    psum x1 -> x0, waiting for transfers between devices: 90.8 us -> none  [on_device(): total = lax.psum(partial_value, 'mp')]
    reduce_scatter x0 -> x1, waiting for transfers between devices: none -> 26.8 us  [on_device(): lax.psum_scatter(mine.astype(jnp.bfloat16), 'mp', scatter_dimension=1, ti...]
    unnamed x3 -> x1, waiting for transfers between devices: 24.6 us -> 0.02 us
    scatter x1 -> x0, other arithmetic: 14.8 us -> none  [on_device(): jnp.zeros((experts * capacity, width), jnp.bfloat16).at[target].set(normed)]
    scatter x0 -> x1, local copies, waits for them, and re-layouts: none -> 13.8 us  [on_device(): jnp.zeros((experts * capacity, width), jnp.bfloat16).at[target].set(normed)]
    all_to_all x1, blocking collectives: 81.1 us -> 87.9 us  [on_device(): lax.all_to_all(buffer, 'graph', split_axis=0, concat_axis=0, tiled=True)]
    gather x1 -> x2, local copies, waits for them, and re-layouts: 11.2 us -> 16.8 us  [on_device(): mine = back.reshape(-1, width)[target]]
  transfers between devices with their start and end apart: 5 -> 6, of which waited for: 4 -> 5; matrix products, arithmetic and copies ran while one was open for 3% -> 3% of each run, Pallas kernels for 0% -> 0%
where the time goes in v1:
time: 615 us; the launch traced here: 614 us
  waiting for transfers between devices  317 us (52%)
  local copies, waits for them, and re-layouts  99.7 us (16%)
  blocking collectives  87.9 us (14%)
  matrix products  50.9 us (8%)
  starting transfers between devices  26.1 us (4%)
  other arithmetic  18.2 us (3%)
  between operations  14.4 us (2%)
    ppermute x2, waiting for transfers between devices, on_device(): lax.ppermute(total, 'mp', [(dev, dev ^ hop) for dev in range(4)])  170 us
    all_to_all x1, blocking collectives, on_device(): lax.all_to_all(buffer, 'graph', split_axis=0, concat_axis=0, tiled=True)  87.9 us
    all_to_all x1, waiting for transfers between devices, on_device(): lax.all_to_all(produced.astype(jnp.bfloat16), 'graph', split_axis=0, conc...  73 us
    all_to_all x1, waiting for transfers between devices, on_device(): lax.all_to_all(outgoing, 'graph', split_axis=0, concat_axis=0, tiled=True)  47.1 us
    reduce_scatter x1, waiting for transfers between devices, on_device(): lax.psum_scatter(mine.astype(jnp.bfloat16), 'mp', scatter_dimension=1, ti...  26.8 us
    slice x2, local copies, waits for them, and re-layouts, on_device(): gathered[:, :, :local_width].reshape(blocks, -1, local_heads, HEAD_DIM)  20.4 us
    gather x2, local copies, waits for them, and re-layouts, on_device(): mine = back.reshape(-1, width)[target]  16.8 us
    dot_general x1, matrix products, make_work(): jnp.einsum('gesf,efd->gesd', hidden, down_weights, preferred_element_type...  14.1 us
  transfers between devices with their start and end apart: 6, of which 5 were waited for; matrix products, arithmetic and copies ran while one was open for 3% of the time, Pallas kernels for 0%

profile of v1, /device:TPU:1, one launch (start us, length us, event | category | flops | bytes accessed | tf_op | source)
XLA Modules:
  0.0 613.8 jit_solution(4490984794122186038)
XLA Ops:
  10.1 9.6 %all-to-all-start = ((s32[32,1,2]{2,1,0:T(1,128)}), s32[32,1,2]{2,1,0:T(1,128)S(1)}, u32[]{:S(2)}, u32[]{:S(2)}) async-start(s32[32,1,2]{2,1,0:T(1,128)} %copy.66), calls=%async_computation | async-start | bytes 32768 | tf_op jit(solution)/shard_map/all_to_all | solution.py:77
  20.8 2.3 convolution_convert_fusion
  23.2 2.6 multiply_reduce_fusion.2
  27.3 2.8 gather_fusion
  30.1 7.6 %all-to-all-start.1 = ((bf16[32,2,128,256]{3,2,1,0:T(8,128)(2,1)}), bf16[32,2,128,256]{3,2,1,0:T(8,128)(2,1)}, u32[]{:S(2)}, u32[]{:S(2)}) async-start(bf16[32,2,128,256]{3,2,1,0:T(8,128)(2,1)} %bitcast.144), calls=%async_computation.1 | async-start | bytes 8388608 | tf_op jit(solution)/shard_map/all_to_all | solution.py:79
  40.6 47.1 %all-to-all-done.1 = bf16[32,2,128,256]{3,2,1,0:T(8,128)(2,1)} async-done(((bf16[32,2,128,256]{3,2,1,0:T(8,128)(2,1)}), bf16[32,2,128,256]{3,2,1,0:T(8,128)(2,1)}, u32[]{:S(2)}, u32[]{:S(2)}) %all-to-all-start.1) | async-done | bytes 4194336 | tf_op jit(solution)/shard_map/all_to_all | solution.py:79
  87.8 5.5 pad_maximum_fusion
  93.3 10.7 %gather_fusion.1 = bf16[192,128,256]{2,1,0:T(8,128)(2,1)} fusion(bf16[80,128,256]{2,1,0:T(8,128)(2,1)} %pad_maximum_fusion, s32[1024]{0:T(1024)S(1)} %pad_clamp_fusion), kind=kCustom, calls=%fused_computation.1 | custom fusion | bytes 25166592 | tf_op jit(solution)/shard_map/gather | solution.py:92
  104.1 11.7 %fusion.71 = (bf16[16,1536,128]{2,1,0:T(8,128)(2,1)}, bf16[16,1536,128]{2,1,0:T(8,128)(2,1)}) fusion(bf16[16,1536,256]{2,1,0:T(8,128)(2,1)} %bitcast.142), kind=kLoop, calls=%fused_computation.114 | loop fusion | bytes 25165824 | tf_op jit(solution)/shard_map/slice | solution.py:93
  115.8 8.7 %copy.72 = bf16[16,1536,128]{1,2,0:T(8,128)(2,1)} copy(bf16[16,1536,128]{2,1,0:T(8,128)(2,1)} %get-tuple-element.15) | data formatting | bytes 12582912 | tf_op jit(solution)/shard_map/slice | solution.py:93
  124.4 8.6 %copy.70 = bf16[16,1536,128]{1,2,0:T(8,128)(2,1)} copy(bf16[16,1536,128]{2,1,0:T(8,128)(2,1)} %get-tuple-element.16) | data formatting | bytes 12582912 | tf_op jit(solution)/shard_map/slice | solution.py:94
  133.1 7.8 %fusion.72 = f32[16,2,128]{2,1,0:T(2,128)S(1)} fusion(bf16[16,1536,2,64]{1,3,2,0:T(8,128)(2,1)} %bitcast.145, f32[2048,2,64]{0,2,1:T(8,128)} %get-tuple-element.24, f32[2]{0:T(128)S(1)} %broadcast_multiply_fusion, f32[2048,2]{0,1:T(2,128)S(1)} %add_rsqrt_fusion), kind=kOutput, calls=%fused_computation.115 | convolution fusion | flops 818677248 | bytes 7372808 | tf_op jit(solution)/shard_map/sub | solution.py:100
  140.9 12.9 %fusion.29 = bf16[16,128,2,64]{1,3,2,0:T(8,128)(2,1)} fusion(bf16[16,1536,2,64]{1,3,2,0:T(8,128)(2,1)} %bitcast.147, f32[16,2,128]{2,1,0:T(2,128)S(1)} %fusion.72, bf16[16,1536,2,64]{1,3,2,0:T(8,128)(2,1)} %bitcast.146, f32[2048,2,64]{0,2,1:T(8,128)} %get-tuple-element.24, f32[2]{0:T(128)S(1)} %broadcast_multiply_fusion, f32[2048,2]{0,1:T(2,128)S(1)} %add_rsqrt_fusion), kind=kOutput, calls=%fused_computation.39 | convolution fusion | flops 1630541312 | bytes 14188552 | tf_op jit(solution)/shard_map/bhqk,bkhd->bqhd/dot_general | solution.py:102
  157.2 87.2 %collective-permute-done = f32[2048,512]{0,1:T(8,128)S(1)} collective-permute-done((f32[2048,512]{0,1:T(8,128)S(1)}, f32[2048,512]{0,1:T(8,128)S(1)}, u32[]{:S(2)}, u32[]{:S(2)}) %collective-permute-start) | collective-permute-done | bytes 4194336 | tf_op jit(solution)/shard_map/ppermute | solution.py:109
  244.4 2.7 add.143
  247.1 2.7 collective-permute-start.1
  249.9 2.5 copy.75
  254.1 82.4 %collective-permute-done.1 = f32[2048,512]{0,1:T(8,128)} collective-permute-done((f32[2048,512]{0,1:T(8,128)}, f32[2048,512]{0,1:T(8,128)}, u32[]{:S(2)}, u32[]{:S(2)}) %collective-permute-start.1) | collective-permute-done | bytes 4194336 | tf_op jit(solution)/shard_map/ppermute | solution.py:109
  336.5 6.1 multiply_reduce_fusion
  345.0 2.5 copy.76
  347.5 13.8 %scatter_custom_fusion = bf16[6144,512]{1,0:T(8,128)(2,1)} fusion(s32[2048]{0:T(1024)S(1)} %bitcast.157, bf16[2048,512]{1,0:T(8,128)(2,1)} %copy.76, bf16[]{:T(256)} %constant.85.clone.1), kind=kCustom, calls=%fused_computation.28 | custom fusion | bytes 6291968 | tf_op jit(solution)/shard_map/scatter | solution.py:125
  361.3 87.9 %all_to_all.21 = bf16[32,2,96,512]{3,2,1,0:T(8,128)(2,1)S(1)} all-to-all(bf16[32,2,96,512]{3,2,1,0:T(8,128)(2,1)} %bitcast.143), channel_id=1, replica_groups=mesh['graph'=32,'mp'=4] {'graph'}, dimensions={0} | all-to-all | bytes 12582912 | tf_op jit(solution)/shard_map/all_to_all | solution.py:131
  449.2 2.6 copy-done.2
  451.7 6.4 %fusion.9 = f32[2,32,96,512]{3,2,1,0:T(8,128)} fusion(bf16[32,2,96,512]{3,2,1,0:T(8,128)(2,1)S(1)} %all_to_all.21, bf16[2,512,512]{2,1,0:T(8,128)(2,1)S(1)} %copy-done), kind=kOutput, calls=%fused_computation.20 | convolution fusion | flops 3221225472 | bytes 19922944 | tf_op jit(solution)/shard_map/gesd,edf->gesf/dot_general | solution.py:20
  458.2 14.1 %convert_bitcast_fusion = bf16[32,2,96,512]{3,2,0,1:T(8,128)(2,1)} fusion(f32[2,32,96,512]{3,2,1,0:T(8,128)} %fusion.9, bf16[32,2,96,512]{3,2,1,0:T(8,128)(2,1)} %copy-done.2, bf16[2,512,512]{2,1,0:T(8,128)(2,1)} %param.19, bf16[2,512,512]{2,1,0:T(8,128)(2,1)} %param.17), kind=kOutput, calls=%fused_computation.18 | convolution fusion | flops 6464471040 | bytes 27262976 | tf_op jit(solution)/shard_map/gesf,efd->gesd/dot_general | solution.py:22
  472.3 6.2 %copy.79 = bf16[32,2,96,512]{3,2,1,0:T(8,128)(2,1)} copy(bf16[32,2,96,512]{3,2,0,1:T(8,128)(2,1)} %convert_bitcast_fusion) | data formatting | bytes 12582912 | tf_op jit(solution)/shard_map/convert_element_type | solution.py:134
  478.5 4.9 all-to-all-start.3
  483.4 73.0 %all-to-all-done.3 = bf16[32,2,96,512]{3,2,1,0:T(8,128)(2,1)} async-done(((bf16[32,2,96,512]{3,2,1,0:T(8,128)(2,1)}), bf16[32,2,96,512]{3,2,1,0:T(8,128)(2,1)}, u32[]{:S(2)}, u32[]{:S(2)}) %all-to-all-start.3) | async-done | bytes 6291488 | tf_op jit(solution)/shard_map/all_to_all | solution.py:133
  556.4 12.8 %gather_fusion.2 = bf16[2048,512]{1,0:T(8,128)(2,1)} fusion(bf16[6144,512]{1,0:T(8,128)(2,1)} %bitcast.116, s32[2048]{0:T(1024)S(1)} %broadcast_clamp_fusion), kind=kCustom, calls=%fused_computation.2 | custom fusion | bytes 4202496 | tf_op jit(solution)/shard_map/gather | solution.py:136
  569.2 4.0 copy.80
  575.1 2.0 copy.81
  577.7 26.8 %reduce-scatter.2.cloned.1.call-done = bf16[2048,128]{0,1:T(8,128)(2,1)} async-done(((bf16[2048,512]{0,1:T(8,128)(2,1)}), bf16[2048,128]{0,1:T(8,128)(2,1)}) %reduce-scatter.2.cloned.1.call-update) | async-done | bytes 524304 | tf_op jit(solution)/shard_map/reduce_scatter | solution.py:137
  (84 shorter events, 20.8 us)
Async XLA Ops:
  7.2 444.6 %copy-start = (bf16[2,512,512]{2,1,0:T(8,128)(2,1)S(1)}, bf16[2,512,512]{2,1,0:T(8,128)(2,1)}, u32[]{:S(2)}) copy-start(bf16[2,512,512]{2,1,0:T(8,128)(2,1)} %param.18) | copy-start | bytes 3145732
  10.1 16.6 %all-to-all-start = ((s32[32,1,2]{2,1,0:T(1,128)}), s32[32,1,2]{2,1,0:T(1,128)S(1)}, u32[]{:S(2)}, u32[]{:S(2)}) async-start(s32[32,1,2]{2,1,0:T(1,128)} %copy.66), calls=%async_computation | async-start | bytes 32768 | tf_op jit(solution)/shard_map/all_to_all | solution.py:77
  23.1 3.7 copy-start.6
  26.5 0.8 copy-start.5
  30.0 7.6 %copy-start.10 = (s32[16,12]{1,0:T(8,128)S(1)}, s32[16,12]{1,0:T(8,128)}, u32[]{:S(2)}) copy-start(s32[16,12]{1,0:T(8,128)} %param.20) | copy-start | bytes 2308
  30.0 8.7 %copy-start.12 = (f32[2]{0:T(128)S(1)}, f32[2]{0:T(128)}, u32[]{:S(2)}) copy-start(f32[2]{0:T(128)} %param.14) | copy-start | bytes 28
  30.1 8.7 %copy-start.1 = (bf16[2048,512]{1,0:T(8,128)(2,1)S(1)}, bf16[2048,512]{1,0:T(8,128)(2,1)}, u32[]{:S(2)}) copy-start(bf16[2048,512]{1,0:T(8,128)(2,1)} %param.11) | copy-start | bytes 6291460
  30.1 57.7 %all-to-all-start.1 = ((bf16[32,2,128,256]{3,2,1,0:T(8,128)(2,1)}), bf16[32,2,128,256]{3,2,1,0:T(8,128)(2,1)}, u32[]{:S(2)}, u32[]{:S(2)}) async-start(bf16[32,2,128,256]{3,2,1,0:T(8,128)(2,1)} %bitcast.144), calls=%async_computation.1 | async-start | bytes 8388608 | tf_op jit(solution)/shard_map/all_to_all | solution.py:79
  140.9 14.3 %copy-start.7 = (bf16[128,512]{1,0:T(8,128)(2,1)S(1)}, bf16[128,512]{1,0:T(8,128)(2,1)}, u32[]{:S(2)}) copy-start(bf16[128,512]{1,0:T(8,128)(2,1)} %param.13) | copy-start | bytes 393220
  155.9 96.5 %copy-start.9 = (s32[2048,1]{0,1:T(1,128)S(1)}, s32[2048,1]{0,1:T(1,128)}, u32[]{:S(2)}) copy-start(s32[2048,1]{0,1:T(1,128)} %param.21) | copy-start | bytes 24580
  155.9 88.5 %collective-permute-start = (f32[2048,512]{0,1:T(8,128)S(1)}, f32[2048,512]{0,1:T(8,128)S(1)}, u32[]{:S(2)}, u32[]{:S(2)}) collective-permute-start(f32[2048,512]{0,1:T(8,128)S(1)} %fusion.37), channel_id=1, source_target_pairs={{0,1},{1,0},{2,3},{3,2},{4,5},{5,4},{6,7},{7,6},{8,9},{9,8},{10,11... | collective-permute-start | bytes 12582920 | tf_op jit(solution)/shard_map/ppermute | solution.py:109
  247.1 89.3 %collective-permute-start.1 = (f32[2048,512]{0,1:T(8,128)}, f32[2048,512]{0,1:T(8,128)}, u32[]{:S(2)}, u32[]{:S(2)}) collective-permute-start(f32[2048,512]{0,1:T(8,128)} %add.143), channel_id=1, source_target_pairs={{0,2},{1,3},{2,0},{3,1},{4,6},{5,7},{6,4},{7,5},{8,10},{9,11},{10,... | collective-permute-start | bytes 12582920 | tf_op jit(solution)/shard_map/ppermute | solution.py:109
  252.4 84.1 %copy-start.4 = (bf16[2048,512]{0,1:T(8,128)(2,1)S(1)}, bf16[2048,512]{0,1:T(8,128)(2,1)}, u32[]{:S(2)}) copy-start(bf16[2048,512]{0,1:T(8,128)(2,1)} %copy.75) | copy-start | bytes 6291460
  254.1 90.5 %copy-start.11 = (f32[512]{0:T(512)S(1)}, f32[512]{0:T(512)}, u32[]{:S(2)}) copy-start(f32[512]{0:T(512)} %param.15) | copy-start | bytes 6148
  342.6 2.0 copy-start.3
  449.2 2.6 copy-start.2
  478.5 77.9 %all-to-all-start.3 = ((bf16[32,2,96,512]{3,2,1,0:T(8,128)(2,1)}), bf16[32,2,96,512]{3,2,1,0:T(8,128)(2,1)}, u32[]{:S(2)}, u32[]{:S(2)}) async-start(bf16[32,2,96,512]{3,2,1,0:T(8,128)(2,1)} %copy.79), calls=%async_computation.3 | async-start | bytes 12582912 | tf_op jit(solution)/shard_map/all_to_all | solution.py:133
  483.4 121.1 %reduce-scatter.2.cloned.1.call-start = ((), (), s32[]{:S(2)}) async-start(), calls=%async_computation.5 | async-start | bytes 2621440 | tf_op jit(solution)/shard_map/reduce_scatter | solution.py:137
  569.2 8.0 %copy-start.8 = (bf16[512,64]{0,1:T(8,128)(2,1)S(1)}, bf16[512,64]{0,1:T(8,128)(2,1)}, u32[]{:S(2)}) copy-start(bf16[512,64]{0,1:T(8,128)(2,1)} %param.16) | copy-start | bytes 196612
Sparse Core Ops, SparseCore 0:
  573.4 31.0 reduce-scatter.1
